TPU v7x, 32 devices: a whole 2x2x4 slice. The times are simulated.
32 devices in a mesh: groups: 2 (over y), wide: 4 (over z), narrow: 2 (over x), sub: 2 (over core).
Axes of the slice: x: 2, y: 2, z: 4, core: 2. Of those that a mesh axis runs over, the one named last changes fastest.
Arguments:
- amplitudes: bfloat16 [4, 2048, 7680], P(('narrow', 'sub'), 'groups', 'wide'), parts along dimension 1, may hold values from -6 to 6
- integrals: bfloat16 [4, 4, 48, 256, 256], P(('narrow', 'sub'), 'wide'), may hold values from -0.09375 to 0.09375
- tile_list: int32 [4, 4, 48, 2], P(('narrow', 'sub'), 'wide'), may hold values from 0 to 29, as said below
- tile_counts: int32 [4, 4], P(('narrow', 'sub'), 'wide'), may hold values from 12 to 48, as said below
Outputs:
- ladder: float32 [2048, 15360], P(('groups', 'narrow', 'sub'), 'wide'), parts along dimension 0
There are 2 independent parts, one for each index of `groups`. A program takes and returns all parts, laid end to end along the dimension named above; an argument that names none is the same for every part. Nothing has to cross between parts.
Inputs may be any that keep to these rules, and one draw needn't show every extreme that they name: `tile_list`: slots of one device name distinct tiles; entry 0 is a row block below 30, entry 1 a column block below 15; slots at or past the device's count are not part of the sum. `tile_counts`: some device holds 48 live slots in every draw.
All inputs are finite; a program needn't handle non-finite values.
Results may differ from a plain program's by a relative error of at most 0.0003.
Values may be sent and summed in bfloat16 or wider, within the bound.
A program may use at most 128 MiB of HBM per device.

v0:
```python
import jax
import jax.numpy as jnp
from jax import lax
from jax.sharding import PartitionSpec as P

CB_DEV = 15


def group_width(slot_count):
    best = 1
    for candidate in range(1, 9):
        if slot_count % candidate == 0:
            best = candidate
    return best


def shards(amplitudes, integrals, tile_list, tile_counts):
    gathered = lax.all_gather(amplitudes[0], "wide", axis=1, tiled=True)
    tile_block = integrals[0, 0]
    listed = tile_list[0, 0]
    live_count = tile_counts[0, 0]
    slab_rows = gathered.shape[0]
    block_size = tile_block.shape[1]
    slot_count = tile_block.shape[0]
    row_blocks = gathered.shape[1] // block_size
    blocks = gathered.reshape(slab_rows, row_blocks, block_size)
    width = group_width(slot_count)
    group_total = (live_count + width - 1) // width

    def add_group(group_index, total):
        first = group_index * width
        these = lax.dynamic_slice_in_dim(listed, first, width, 0)
        tiles_here = lax.dynamic_slice_in_dim(tile_block, first, width, 0)
        chosen = jnp.take(blocks, these[:, 0], axis=1)
        products = jnp.einsum(
            "stp,tpq->tsq", chosen, tiles_here, preferred_element_type=jnp.float32
        )
        live = (first + jnp.arange(width) < live_count).astype(jnp.float32)
        for member in range(width):
            column_start = these[member, 1] * block_size
            current = lax.dynamic_slice_in_dim(total, column_start, block_size, 1)
            updated = current + products[member] * live[member]
            total = lax.dynamic_update_slice_in_dim(total, updated, column_start, 1)
        return total

    empty = jnp.zeros((slab_rows, CB_DEV * block_size), jnp.float32)
    partial_value = lax.fori_loop(0, group_total, add_group, empty)
    result = lax.psum_scatter(partial_value, ("narrow", "sub"), scatter_dimension=0, tiled=True)
    return result


def solution(mesh):
    placed = (
        P(("narrow", "sub"), "groups", "wide"),
        P(("narrow", "sub"), "wide", None, None, None),
        P(("narrow", "sub"), "wide", None, None),
        P(("narrow", "sub"), "wide"),
    )
    return jax.shard_map(
        shards,
        mesh=mesh,
        in_specs=placed,
        out_specs=P(("groups", "narrow", "sub"), "wide"),
        check_vma=False,
    )
```

profile of v0, /device:TPU:0, one launch (start us, length us, event | category | flops | bytes accessed | tf_op | source)
XLA Modules:
  0.0 702.5 jit_solution(9721475943837812323)
XLA Ops:
  6.5 0.0 all-gather.3.cloned.1.call-start
  6.5 6.3 copy.6
  12.8 0.0 all-gather.3.cloned.1.call-update
  12.8 0.0 reduce-scatter.2.cloned.1.call-start
  13.5 271.8 %all-gather.3.cloned.1.call-done = bf16[1,1024,7680]{1,2,0:T(8,128)(2,1)} async-done(((bf16[1,1024,1920]{1,2,0:T(8,128)(2,1)}), bf16[1,1024,7680]{1,2,0:T(8,128)(2,1)}) %all-gather.3.cloned.1.call-update) | async-done | bytes 15728656 | tf_op jit(solution)/shard_map/all_gather | solution.py:18
  285.3 20.7 %copy.7 = bf16[1024,30,256]{2,0,1:T(8,128)(2,1)} copy(bf16[1024,30,256]{0,2,1:T(8,128)(2,1)} %bitcast.130) | data formatting | bytes 31457280 | tf_op jit(solution)/shard_map/while | solution.py:47
  306.0 0.0 copy-start
  306.0 6.5 broadcast_in_dim.13
  312.5 0.0 copy-done
  312.5 88.2 %while.10 = (s32[]{:T(128)}, f32[1024,3840]{1,0:T(8,128)}, s32[]{:T(128)}, s32[48,2]{0,1:T(2,128)S(1)}, bf16[1024,30,256]{2,0,1:T(8,128)(2,1)}, /*index=5*/bf16[...) while((s32[]{:T(128)}, f32[1024,3840]{1,0:T(8,128)}, ...), condition=%wide.region_1.2_spmd, body=%wide.region_0.1_spmd.sunk | while | flops 1080034432 | bytes 47195148 | solution.py:47
  312.5 0.6 compare_convert_fusion.2
  313.2 0.1 constant_dynamic-slice_fusion.2
  313.3 0.7 fusion.51
  319.2 0.7 fusion.54
  319.9 8.3 %gather_fusion = bf16[8,1024,256]{2,1,0:T(8,128)(2,1)} fusion(bf16[1024,30,256]{2,0,1:T(8,128)(2,1)} %get-tuple-element.187, s32[1024]{0:T(1024)S(1)} %pad_clamp_fusion.2), kind=kCustom, calls=%fused_computation.clone.1 | custom fusion | bytes 8388640 | tf_op jit(solution)/shard_map/while/body/jit(_take)/gather | solution.py:34
  328.1 3.8 fusion.53
  331.9 3.1 fusion.55
  335.0 3.1 fusion.56
  338.1 3.1 fusion.57
  341.2 3.1 fusion.58
  344.3 3.1 fusion.59
  347.4 3.2 fusion.60
  350.6 3.1 fusion.61
  353.7 3.1 fusion.62
  356.8 0.6 compare_convert_fusion.2
  357.4 0.1 constant_dynamic-slice_fusion.2
  357.5 0.7 fusion.51
  363.4 0.7 fusion.54
  364.1 8.3 %gather_fusion = bf16[8,1024,256]{2,1,0:T(8,128)(2,1)} fusion(bf16[1024,30,256]{2,0,1:T(8,128)(2,1)} %get-tuple-element.187, s32[1024]{0:T(1024)S(1)} %pad_clamp_fusion.2), kind=kCustom, calls=%fused_computation.clone.1 | custom fusion | bytes 8388640 | tf_op jit(solution)/shard_map/while/body/jit(_take)/gather | solution.py:34
  372.4 3.8 fusion.53
  376.2 3.1 fusion.55
  379.2 3.1 fusion.56
  382.4 3.1 fusion.57
  385.4 3.1 fusion.58
  388.5 3.0 fusion.59
  391.5 3.0 fusion.60
  394.6 3.1 fusion.61
  397.6 3.1 fusion.62
  400.7 0.0 reduce-scatter.2.cloned.1.call-update
  400.7 295.0 %reduce-scatter.2.cloned.1.call-done = f32[256,3840]{1,0:T(8,128)} async-done(((f32[1024,3840]{1,0:T(8,128)}), f32[256,3840]{1,0:T(8,128)}) %reduce-scatter.2.cloned.1.call-update) | async-done | bytes 3932176 | tf_op jit(solution)/shard_map/reduce_scatter | solution.py:48
  (6 shorter events, 0.0 us)
Async XLA Ops:
  6.5 278.8 %all-gather.3.cloned.1.call-start = ((), (), s32[]{:S(2)}) async-start(), calls=%async_computation.2 | async-start | bytes 19660800 | tf_op jit(solution)/shard_map/all_gather | solution.py:18
  12.8 682.8 %reduce-scatter.2.cloned.1.call-start = ((), (), s32[]{:S(2)}) async-start(), calls=%async_computation.1 | async-start | bytes 19660800 | tf_op jit(solution)/shard_map/reduce_scatter | solution.py:48
  306.0 6.5 copy-start
Sparse Core Ops, SparseCore 0:
  12.9 272.3 all-gather.2
  400.8 294.7 reduce-scatter.1
where the time goes:
time: 706 us; the launch traced here: 702 us
  waiting for transfers between devices  567 us (80%)
  local copies, waits for them, and re-layouts  52.9 us (7%)
  other arithmetic  50.6 us (7%)
  between operations  14.1 us (2%)
  loops' own time  10.5 us (1%)
  matrix products  7.57 us (1%)
    reduce_scatter x1, waiting for transfers between devices, shards(): lax.psum_scatter(partial_value, ('narrow', 'sub'), scatter_dimension=0, t...  295 us
    all_gather x1, waiting for transfers between devices, shards(): gathered = lax.all_gather(amplitudes[0], 'wide', axis=1, tiled=True)  272 us
    dynamic_update_slice x16, other arithmetic, add_group(): total = lax.dynamic_update_slice_in_dim(total, updated, column_start, 1)  49.3 us
    while x1, local copies, waits for them, and re-layouts, shards(): partial_value = lax.fori_loop(0, group_total, add_group, empty)  20.7 us
    gather x2, local copies, waits for them, and re-layouts, add_group(): chosen = jnp.take(blocks, these[:, 0], axis=1)  16.5 us
  transfers between devices with their start and end apart: 2, of which 2 were waited for; matrix products, arithmetic and copies ran while one was open for 0% of the time, Pallas kernels for 0%

commit v1 on v0

--- a/solution.py
+++ b/solution.py
@@ -1,9 +1,15 @@
+import functools
+
 import jax
 import jax.numpy as jnp
 from jax import lax
+from jax.experimental import pallas as pl
+from jax.experimental.pallas import tpu as pltpu
 from jax.sharding import PartitionSpec as P
 
 CB_DEV = 15
+CHUNKS = 8
+MESH = pl.DeviceIdType.MESH
 
 
 def group_width(slot_count):
@@ -14,7 +20,7 @@
     return best
 
 
-def shards(amplitudes, integrals, tile_list, tile_counts):
+def gathered_shards(amplitudes, integrals, tile_list, tile_counts):
     gathered = lax.all_gather(amplitudes[0], "wide", axis=1, tiled=True)
     tile_block = integrals[0, 0]
     listed = tile_list[0, 0]
@@ -49,6 +55,267 @@
     return result
 
 
+def tile_order(listed, live_count):
+    count = listed.shape[0]
+    place = jnp.arange(count, dtype=jnp.int32)
+    column = jnp.where(place < live_count, listed[:, 1], CB_DEV)
+    key = column * count + place
+    rank = jnp.sum((key[None, :] < key[:, None]).astype(jnp.int32), axis=1)
+    at = (rank[None, :] == place[:, None]).astype(jnp.int32)
+    order = jnp.sum(at * place[None, :], axis=1)
+    rows = jnp.sum(at * listed[None, :, 0], axis=1)
+    first = jnp.sum((column[None, :] < column[:, None]).astype(jnp.int32), axis=1)
+    keep = jnp.sum(at * (first != rank).astype(jnp.int32)[None, :], axis=1)
+    columns = jnp.arange(CB_DEV, dtype=jnp.int32)
+    here = jnp.sum((column[None, :] == columns[:, None]).astype(jnp.int32), axis=1)
+    upto = jnp.sum((column[None, :] <= columns[:, None]).astype(jnp.int32), axis=1)
+    last = jnp.where(here > 0, upto - 1, count)
+    return order, rows, keep, last
+
+
+def ladder_kernel(
+    n_wide,
+    order, rows_of, keep, last, amp, tiles, out,
+    held, mine, tile_held, sums, first_out, first_in, total, second_out, second_in,
+    own_sem, tile_sem, left_sem, right_sem, come_sem,
+    first_send, first_recv, second_send, second_recv, out_sem,
+):
+    w = lax.axis_index("wide")
+    n = lax.axis_index("narrow")
+    s = lax.axis_index("sub")
+    quarters, quarter_rows, piece = amp.shape
+    step = quarter_rows // CHUNKS
+    slots, block, _ = tiles.shape
+    strips = n_wide * piece // 128
+    per_block = block // 128
+
+    barrier = pltpu.get_barrier_semaphore()
+    pl.semaphore_signal(barrier, inc=1, device_id={"sub": 1 - s}, device_id_type=MESH)
+    pl.semaphore_signal(barrier, inc=1, device_id={"narrow": 1 - n}, device_id_type=MESH)
+
+    @pl.when(w > 0)
+    def _():
+        pl.semaphore_signal(barrier, inc=1, device_id={"wide": w - 1}, device_id_type=MESH)
+
+    @pl.when(w < n_wide - 1)
+    def _():
+        pl.semaphore_signal(barrier, inc=1, device_id={"wide": w + 1}, device_id_type=MESH)
+
+    own_copy = pltpu.make_async_copy(
+        amp, held.at[:, :, pl.ds(pl.multiple_of(w * piece, 128), piece)], own_sem
+    )
+    own_copy.start()
+    tile_copy = pltpu.make_async_copy(tiles, tile_held, tile_sem)
+    tile_copy.start()
+    sums[slots] = jnp.zeros(sums.shape[1:], jnp.float32)
+
+    at_end = (w == 0) | (w == n_wide - 1)
+    pl.semaphore_wait(barrier, jnp.where(at_end, 3, 4) if n_wide > 1 else 2)
+
+    def some(c):
+        return pl.ds(pl.multiple_of(c * step, step), step)
+
+    def part(origin, c):
+        return held.at[:, some(c), pl.ds(pl.multiple_of(origin * piece, 128), piece)]
+
+    def to_left(origin, c, source=None):
+        return pltpu.make_async_remote_copy(
+            src_ref=part(origin, c) if source is None else source,
+            dst_ref=part(origin, c),
+            send_sem=left_sem.at[origin, c],
+            recv_sem=come_sem.at[origin, c],
+            device_id={"wide": w - 1},
+            device_id_type=MESH,
+        )
+
+    def to_right(origin, c, source=None):
+        return pltpu.make_async_remote_copy(
+            src_ref=part(origin, c) if source is None else source,
+            dst_ref=part(origin, c),
+            send_sem=right_sem.at[origin, c],
+            recv_sem=come_sem.at[origin, c],
+            device_id={"wide": w + 1},
+            device_id_type=MESH,
+        )
+
+    def send_own(c):
+        @pl.when(w > 0)
+        def _():
+            to_left(w, c, amp.at[:, some(c), :]).start()
+
+        @pl.when(w < n_wide - 1)
+        def _():
+            to_right(w, c, amp.at[:, some(c), :]).start()
+
+    def first_copy(c):
+        return pltpu.make_async_remote_copy(
+            src_ref=first_out.at[c],
+            dst_ref=first_in.at[c],
+            send_sem=first_send.at[c],
+            recv_sem=first_recv.at[c],
+            device_id={"sub": 1 - s},
+            device_id_type=MESH,
+        )
+
+    def second_copy(c):
+        return pltpu.make_async_remote_copy(
+            src_ref=second_out.at[c],
+            dst_ref=second_in.at[c],
+            send_sem=second_send.at[c],
+            recv_sem=second_recv.at[c],
+            device_id={"narrow": 1 - n},
+            device_id_type=MESH,
+        )
+
+    def out_copy(c):
+        return pltpu.make_async_copy(second_in.at[c], out.at[some(c), :], out_sem.at[c])
+
+    send_own(0)
+    send_own(1)
+    own_copy.wait()
+    tile_copy.wait()
+
+    def turn(c, nothing):
+        @pl.when(c < CHUNKS)
+        def _():
+            @pl.when(c + 2 < CHUNKS)
+            def _():
+                send_own(c + 2)
+
+            for distance in range(1, n_wide):
+                @pl.when(w + distance < n_wide)
+                def _():
+                    to_left(w + distance, c).wait_recv()
+
+                    @pl.when(w > 0)
+                    def _():
+                        to_left(w + distance, c).start()
+
+                @pl.when(w - distance >= 0)
+                def _():
+                    to_right(w - distance, c).wait_recv()
+
+                    @pl.when(w < n_wide - 1)
+                    def _():
+                        to_right(w - distance, c).start()
+
+            for half in range(2):
+                for place, quarter in ((half, 2 * half + 1 - s), (2 + half, 2 * half + s)):
+                    for strip in range(strips):
+                        mine[strip, place] = held[quarter, some(c), pl.ds(strip * 128, 128)]
+
+            def multiply(t, so_far):
+                chosen = jnp.concatenate(
+                    [
+                        mine[rows_of[t] * per_block + strip].reshape(quarters * step, 128)
+                        for strip in range(per_block)
+                    ],
+                    axis=1,
+                )
+                product = jnp.dot(
+                    chosen, tile_held[order[t]], preferred_element_type=jnp.float32
+                )
+                so_far = so_far * keep[t].astype(jnp.float32) + product
+                sums[t] = so_far.reshape(quarters, step, block)
+                return so_far
+
+            lax.fori_loop(
+                0, slots, multiply, jnp.zeros((quarters * step, block), jnp.float32)
+            )
+
+            slot = lax.rem(c, 3)
+            for b in range(CB_DEV):
+                columns = pl.ds(b * block, block)
+                column_sum = sums[last[b]]
+                first_out[c, :, :, columns] = column_sum[:2]
+                total[slot, :, :, columns] = column_sum[2:]
+            first_copy(c).start()
+
+        @pl.when((c >= 1) & (c <= CHUNKS))
+        def _():
+            e = c - 1
+            slot = lax.rem(e, 3)
+            first_copy(e).wait_recv()
+            second_out[e] = total[slot, 1 - n] + first_in[e, 1 - n]
+            second_copy(e).start()
+            total[slot, n] = total[slot, n] + first_in[e, n]
+
+        @pl.when(c >= 2)
+        def _():
+            e = c - 2
+            second_copy(e).wait_recv()
+            second_in[e] = second_in[e] + total[lax.rem(e, 3), n]
+            out_copy(e).start()
+
+        return nothing
+
+    lax.fori_loop(0, CHUNKS + 2, turn, 0)
+
+    def finish(c, nothing):
+        for origin in range(n_wide):
+            @pl.when((w > 0) & (origin >= w))
+            def _():
+                to_left(origin, c).wait_send()
+
+            @pl.when((w < n_wide - 1) & (origin <= w))
+            def _():
+                to_right(origin, c).wait_send()
+
+        first_copy(c).wait_send()
+        second_copy(c).wait_send()
+        out_copy(c).wait()
+        return nothing
+
+    lax.fori_loop(0, CHUNKS, finish, 0)
+
+
+def fused_shards(n_wide, amplitudes, integrals, tile_list, tile_counts):
+    _, slab_rows, piece = amplitudes.shape
+    slots, block = integrals.shape[2], integrals.shape[3]
+    quarter_rows = slab_rows // 4
+    step = quarter_rows // CHUNKS
+    width = CB_DEV * block
+    ordered = tile_order(tile_list[0, 0], tile_counts[0, 0])
+    in_smem = pl.BlockSpec(memory_space=pltpu.SMEM)
+    anywhere = pl.BlockSpec(memory_space=pl.ANY)
+    dma = pltpu.SemaphoreType.DMA
+    return pl.pallas_call(
+        functools.partial(ladder_kernel, n_wide),
+        out_shape=jax.ShapeDtypeStruct((quarter_rows, width), jnp.float32),
+        in_specs=[in_smem] * 4 + [anywhere] * 2,
+        out_specs=anywhere,
+        scratch_shapes=[
+            pltpu.VMEM((4, quarter_rows, n_wide * piece), jnp.bfloat16),
+            pltpu.VMEM((n_wide * piece // 128, 4, step, 128), jnp.bfloat16),
+            pltpu.VMEM((slots, block, block), jnp.bfloat16),
+            pltpu.VMEM((slots + 1, 4, step, block), jnp.float32),
+            pltpu.VMEM((CHUNKS, 2, step, width), jnp.float32),
+            pltpu.VMEM((CHUNKS, 2, step, width), jnp.float32),
+            pltpu.VMEM((3, 2, step, width), jnp.float32),
+            pltpu.VMEM((CHUNKS, step, width), jnp.float32),
+            pltpu.VMEM((CHUNKS, step, width), jnp.float32),
+            dma, dma,
+            dma((n_wide, CHUNKS)), dma((n_wide, CHUNKS)), dma((n_wide, CHUNKS)),
+            dma((CHUNKS,)), dma((CHUNKS,)), dma((CHUNKS,)), dma((CHUNKS,)), dma((CHUNKS,)),
+        ],
+        compiler_params=pltpu.CompilerParams(
+            collective_id=0, has_side_effects=True, vmem_limit_bytes=63 * 1024 * 1024
+        ),
+    )(*ordered, amplitudes.reshape(4, quarter_rows, piece), integrals[0, 0])
+
+
+def shards(sizes, amplitudes, integrals, tile_list, tile_counts):
+    fits = (
+        sizes["narrow"] == 2
+        and sizes["sub"] == 2
+        and sizes["wide"] <= 4
+        and amplitudes.shape[2] % 128 == 0
+    )
+    if fits:
+        return fused_shards(sizes["wide"], amplitudes, integrals, tile_list, tile_counts)
+    return gathered_shards(amplitudes, integrals, tile_list, tile_counts)
+
+
 def solution(mesh):
     placed = (
         P(("narrow", "sub"), "groups", "wide"),
@@ -57,7 +324,7 @@
         P(("narrow", "sub"), "wide"),
     )
     return jax.shard_map(
-        shards,
+        functools.partial(shards, dict(mesh.shape)),
         mesh=mesh,
         in_specs=placed,
         out_specs=P(("groups", "narrow", "sub"), "wide"),

time: 706 us -> 301 us (0.43)
  waiting for transfers between devices: 567 us -> 0 us
  Pallas kernels: 0 us -> 293 us
  local copies, waits for them, and re-layouts: 52.9 us -> 4.29 us
  other arithmetic: 50.6 us -> 2.98 us
  between operations: 14.1 us -> 0.67 us
  loops' own time: 10.5 us -> 0 us
  matrix products: 7.57 us -> 0 us
    reduce_scatter x1 -> x0, waiting for transfers between devices: 295 us -> none  [shards(): lax.psum_scatter(partial_value, ('narrow', 'sub'), scatter_dimension=0, t...]
    pallas_call x0 -> x1, Pallas kernels: none -> 293 us  [fused_shards(): pl.pallas_call(functools.partial(ladder_kernel, n_wide), out_shape=jax.Sh...]
    all_gather x1 -> x0, waiting for transfers between devices: 272 us -> none  [shards(): gathered = lax.all_gather(amplitudes[0], 'wide', axis=1, tiled=True)]
    dynamic_update_slice x16 -> x0, other arithmetic: 49.3 us -> none  [add_group(): total = lax.dynamic_update_slice_in_dim(total, updated, column_start, 1)]
    while x1 -> x0, local copies, waits for them, and re-layouts: 20.7 us -> none  [shards(): partial_value = lax.fori_loop(0, group_total, add_group, empty)]
    gather x2 -> x0, local copies, waits for them, and re-layouts: 16.5 us -> none  [add_group(): chosen = jnp.take(blocks, these[:, 0], axis=1)]
    another operation x1 -> x0, loops' own time: 10.5 us -> none  [shards(): partial_value = lax.fori_loop(0, group_total, add_group, empty)]
    dot_general x2 -> x0, matrix products: 7.57 us -> none  [add_group(): jnp.einsum('stp,tpq->tsq', chosen, tiles_here, preferred_element_type=jnp...]
  transfers between devices with their start and end apart: 2 -> 0, of which waited for: 2 -> 0; matrix products, arithmetic and copies ran while one was open for 0% -> 0% of each run, Pallas kernels for 0% -> 0%
where the time goes in v1:
time: 301 us
  Pallas kernels  293 us (97%)
  local copies, waits for them, and re-layouts  4.29 us (1%)
    pallas_call x1, Pallas kernels, fused_shards(): pl.pallas_call(functools.partial(ladder_kernel, n_wide), out_shape=jax.Sh...  293 us

profile of v1, /device:TPU:0, one launch (start us, length us, event | category | flops | bytes accessed | tf_op | source)
XLA Modules:
  0.0 300.6 jit_solution(9943309899627356395)
XLA Ops:
  0.7 0.7 iota_add_fusion
  1.3 0.8 slice_bitcast_fusion
  2.1 0.2 convert_reduce_fusion
  2.3 0.7 select_reduce_fusion
  3.0 0.1 convert_reduce_fusion.2
  3.1 0.5 compare_select_fusion.last
  3.6 292.7 %shard_map.46 = f32[256,3840]{1,0:T(8,128)} custom-call(s32[48]{0:T(128)} %get-tuple-element.9.order, s32[48]{0:T(128)} %get-tuple-element.8.rows_of, s32[48]{0:T(128)} %get-tuple-element.7.keep, s32[15]{0:T(128)} %compare_select_fusion.last, bf16[4,256,1920]{2,1,0:T(8,128)(2,1)} %bitcast.16, bf16[48,256,256]{2,1,0:T(8,128)(2,1)} %bitcast.15), custom_call_target="tpu_custom_call" | custom-call | tf_op jit(solution)/shard_map/pallas_call | solution.py:282
  296.3 4.3 %copy.7 = f32[256,3840]{1,0:T(8,128)} copy(f32[256,3840]{1,0:T(8,128)} %shard_map.46) | data formatting | bytes 7864320
  (1 shorter events, 0.0 us)

commit v2 on v1

v2 whole, which is shorter than its diff:
```python
import functools

import jax
import jax.numpy as jnp
from jax import lax
from jax.experimental import pallas as pl
from jax.experimental.pallas import tpu as pltpu
from jax.sharding import PartitionSpec as P

CB_DEV = 15
CHUNKS = 8
HOME = 4
UNITS = HOME + 2 * (CHUNKS - HOME)
TILE_PARTS = 4
MESH = pl.DeviceIdType.MESH


def group_width(slot_count):
    best = 1
    for candidate in range(1, 9):
        if slot_count % candidate == 0:
            best = candidate
    return best


def gathered_shards(amplitudes, integrals, tile_list, tile_counts):
    gathered = lax.all_gather(amplitudes[0], "wide", axis=1, tiled=True)
    tile_block = integrals[0, 0]
    listed = tile_list[0, 0]
    live_count = tile_counts[0, 0]
    slab_rows = gathered.shape[0]
    block_size = tile_block.shape[1]
    slot_count = tile_block.shape[0]
    row_blocks = gathered.shape[1] // block_size
    blocks = gathered.reshape(slab_rows, row_blocks, block_size)
    width = group_width(slot_count)
    group_total = (live_count + width - 1) // width

    def add_group(group_index, total):
        first = group_index * width
        these = lax.dynamic_slice_in_dim(listed, first, width, 0)
        tiles_here = lax.dynamic_slice_in_dim(tile_block, first, width, 0)
        chosen = jnp.take(blocks, these[:, 0], axis=1)
        products = jnp.einsum(
            "stp,tpq->tsq", chosen, tiles_here, preferred_element_type=jnp.float32
        )
        live = (first + jnp.arange(width) < live_count).astype(jnp.float32)
        for member in range(width):
            column_start = these[member, 1] * block_size
            current = lax.dynamic_slice_in_dim(total, column_start, block_size, 1)
            updated = current + products[member] * live[member]
            total = lax.dynamic_update_slice_in_dim(total, updated, column_start, 1)
        return total

    empty = jnp.zeros((slab_rows, CB_DEV * block_size), jnp.float32)
    partial_value = lax.fori_loop(0, group_total, add_group, empty)
    result = lax.psum_scatter(partial_value, ("narrow", "sub"), scatter_dimension=0, tiled=True)
    return result


def tile_order(listed, live_count):
    count = listed.shape[0]
    place = jnp.arange(count, dtype=jnp.int32)
    column = jnp.where(place < live_count, listed[:, 1], CB_DEV)
    key = column * count + place
    rank = jnp.sum((key[None, :] < key[:, None]).astype(jnp.int32), axis=1)
    at = (rank[None, :] == place[:, None]).astype(jnp.int32)
    order = jnp.sum(at * place[None, :], axis=1)
    rows = jnp.sum(at * listed[None, :, 0], axis=1)
    first = jnp.sum((column[None, :] < column[:, None]).astype(jnp.int32), axis=1)
    keep = jnp.sum(at * (first != rank).astype(jnp.int32)[None, :], axis=1)
    columns = jnp.arange(CB_DEV, dtype=jnp.int32)
    here = jnp.sum((column[None, :] == columns[:, None]).astype(jnp.int32), axis=1)
    upto = jnp.sum((column[None, :] <= columns[:, None]).astype(jnp.int32), axis=1)
    last = jnp.where(here > 0, upto - 1, count)
    lines = [jnp.pad(line, (0, 128 - line.shape[0])) for line in (order, rows, keep, last)]
    return jnp.pad(jnp.stack(lines), ((0, 4), (0, 0)))


def ladder_kernel(
    n_wide,
    own_list, amp, tiles, list_source, out, list_landed,
    held, mine, own_tiles, end_tiles, end_list, sums,
    first_out, first_in, total, second_out, second_in,
    own_sem, tile_sem, list_sem, left_sem, right_sem, come_sem,
    first_send, first_recv, second_send, second_recv, out_sem,
    part_send, part_recv, across_send, across_recv,
    list_send, list_recv, back_send, back_recv,
):
    g = lax.axis_index("groups")
    w = lax.axis_index("wide")
    n = lax.axis_index("narrow")
    s = lax.axis_index("sub")
    quarters, quarter_rows, piece = amp.shape
    step = quarter_rows // CHUNKS
    slots, block, _ = tiles.shape
    strips = n_wide * piece // 128
    per_block = block // 128
    is_end = (w == 0) | (w == n_wide - 1)
    is_inner = (w > 0) & (w < n_wide - 1)
    mate = w + 1 - 2 * lax.rem(w, 2)
    part_slots = slots // 2 // TILE_PARTS

    barrier = pltpu.get_barrier_semaphore()
    pl.semaphore_signal(barrier, inc=1, device_id={"sub": 1 - s}, device_id_type=MESH)
    pl.semaphore_signal(barrier, inc=1, device_id={"narrow": 1 - n}, device_id_type=MESH)

    @pl.when(is_inner)
    def _():
        pl.semaphore_signal(barrier, inc=1, device_id={"groups": 1 - g}, device_id_type=MESH)

    @pl.when(w > 0)
    def _():
        pl.semaphore_signal(barrier, inc=1, device_id={"wide": w - 1}, device_id_type=MESH)

    @pl.when(w < n_wide - 1)
    def _():
        pl.semaphore_signal(barrier, inc=1, device_id={"wide": w + 1}, device_id_type=MESH)

    own_copy = pltpu.make_async_copy(
        amp, held.at[:, :, pl.ds(pl.multiple_of(w * piece, 128), piece)], own_sem
    )
    own_copy.start()
    tile_copy = pltpu.make_async_copy(tiles, own_tiles, tile_sem)
    tile_copy.start()
    sums[slots] = jnp.zeros(sums.shape[1:], jnp.float32)

    pl.semaphore_wait(barrier, jnp.where(is_end, 3, 5))

    def some(c):
        return pl.ds(pl.multiple_of(c * step, step), step)

    def part(origin, c):
        return held.at[:, some(c), pl.ds(pl.multiple_of(origin * piece, 128), piece)]

    def remote(source, target, send, recv, device):
        return pltpu.make_async_remote_copy(
            src_ref=source, dst_ref=target, send_sem=send, recv_sem=recv,
            device_id=device, device_id_type=MESH,
        )

    def to_left(origin, c, source=None):
        return remote(
            part(origin, c) if source is None else source, part(origin, c),
            left_sem.at[origin, c], come_sem.at[origin, c], {"wide": w - 1},
        )

    def to_right(origin, c, source=None):
        return remote(
            part(origin, c) if source is None else source, part(origin, c),
            right_sem.at[origin, c], come_sem.at[origin, c], {"wide": w + 1},
        )

    def left_takes(c):
        return (w > 1) | ((w == 1) & (c < HOME))

    def right_takes(c):
        return (w < n_wide - 2) | ((w == n_wide - 2) & (c < HOME))

    def send_own(c):
        @pl.when(left_takes(c))
        def _():
            to_left(w, c, amp.at[:, some(c), :]).start()

        @pl.when(right_takes(c))
        def _():
            to_right(w, c, amp.at[:, some(c), :]).start()

    def part_copy(p):
        here = pl.ds(g * (slots // 2) + p * part_slots, part_slots)
        return remote(
            tiles.at[here], end_tiles.at[here], part_send.at[p], part_recv.at[p], {"wide": mate}
        )

    def across_copy(p):
        here = pl.ds(g * (slots // 2) + p * part_slots, part_slots)
        return remote(
            end_tiles.at[here], end_tiles.at[here],
            across_send.at[p], across_recv.at[p], {"groups": 1 - g},
        )

    list_copy = remote(list_source, list_landed, list_send, list_recv, {"wide": mate})

    def first_copy(u):
        return remote(
            first_out.at[lax.rem(u, 2)], first_in.at[u],
            first_send.at[u], first_recv.at[u], {"sub": 1 - s},
        )

    def second_copy(u):
        return remote(
            second_out.at[lax.rem(u, 2)], second_in.at[u],
            second_send.at[u], second_recv.at[u], {"narrow": 1 - n},
        )

    def out_copy(u, c):
        return pltpu.make_async_copy(second_in.at[u], out.at[some(c), :], out_sem.at[c])

    def back_copy(u, c):
        return remote(
            second_in.at[u], out.at[some(c), :], back_send.at[c], back_recv.at[c], {"wide": mate}
        )

    def chunk_of(u):
        return jnp.where(u < HOME, u, lax.div(u, 2) + HOME // 2)

    def active(u):
        return (u >= 0) & ((u < HOME) | (is_inner & (u < UNITS)))

    def for_mate(u):
        return (u >= HOME) & (lax.rem(u, 2) == 0)

    def compute(u, tile_ref, listed):
        def multiply(t, so_far):
            chosen = jnp.concatenate(
                [
                    mine[listed[1, t] * per_block + strip].reshape(quarters * step, 128)
                    for strip in range(per_block)
                ],
                axis=1,
            )
            product = jnp.dot(
                chosen, tile_ref[listed[0, t]], preferred_element_type=jnp.float32
            )
            so_far = so_far * listed[2, t].astype(jnp.float32) + product
            sums[t] = so_far.reshape(quarters, step, block)
            return so_far

        lax.fori_loop(0, slots, multiply, jnp.zeros((quarters * step, block), jnp.float32))
        slot, side = lax.rem(u, 3), lax.rem(u, 2)
        for b in range(CB_DEV):
            columns = pl.ds(b * block, block)
            column_sum = sums[listed[3, b]]
            first_out[side, :, :, columns] = column_sum[:2]
            total[slot, :, :, columns] = column_sum[2:]
        first_copy(u).start()

    send_own(0)

    @pl.when(is_end)
    def _():
        list_copy.start()
        part_copy(0).start()

    send_own(1)
    own_copy.wait()
    tile_copy.wait()

    def turn(u, nothing):
        c = chunk_of(u)
        opens = (u < HOME) | (lax.rem(u, 2) == 0)

        @pl.when(opens & (c + 2 < CHUNKS))
        def _():
            send_own(c + 2)

        @pl.when(is_end & (u + 1 < TILE_PARTS))
        def _():
            part_copy(u + 1).start()

        @pl.when(is_inner & (u >= 1) & (u <= TILE_PARTS))
        def _():
            part_copy(u - 1).wait_recv()
            across_copy(u - 1).start()

        @pl.when(active(u) & opens)
        def _():
            for distance in range(1, n_wide):
                @pl.when(w + distance < n_wide)
                def _():
                    to_left(w + distance, c).wait_recv()

                    @pl.when(left_takes(c))
                    def _():
                        to_left(w + distance, c).start()

                @pl.when(w - distance >= 0)
                def _():
                    to_right(w - distance, c).wait_recv()

                    @pl.when(right_takes(c))
                    def _():
                        to_right(w - distance, c).start()

            for half in range(2):
                for place, quarter in ((half, 2 * half + 1 - s), (2 + half, 2 * half + s)):
                    for strip in range(strips):
                        mine[strip, place] = held[quarter, some(c), pl.ds(strip * 128, 128)]

        @pl.when(is_inner & (u == TILE_PARTS))
        def _():
            list_copy.wait_recv()
            to_list = pltpu.make_async_copy(list_landed, end_list, list_sem)
            to_list.start()
            to_list.wait()
            for p in range(TILE_PARTS):
                across_copy(p).wait_recv()

        @pl.when(active(u) & jnp.logical_not(for_mate(u)))
        def _():
            compute(u, own_tiles, own_list)

        @pl.when(active(u) & for_mate(u))
        def _():
            compute(u, end_tiles, end_list)

        e = u - 1

        @pl.when(active(e))
        def _():
            slot = lax.rem(e, 3)
            first_copy(e).wait()
            second_out[lax.rem(e, 2)] = total[slot, 1 - n] + first_in[e, 1 - n]
            second_copy(e).start()
            total[slot, n] = total[slot, n] + first_in[e, n]

        f = u - 2

        @pl.when(active(f))
        def _():
            second_copy(f).wait()
            second_in[f] = second_in[f] + total[lax.rem(f, 3), n]

            @pl.when(for_mate(f))
            def _():
                back_copy(f, chunk_of(f)).start()

            @pl.when(jnp.logical_not(for_mate(f)))
            def _():
                out_copy(f, chunk_of(f)).start()

        return nothing

    lax.fori_loop(0, UNITS + 2, turn, 0)

    def finish(c, nothing):
        for origin in range(n_wide):
            @pl.when(left_takes(c) & (origin >= w))
            def _():
                to_left(origin, c).wait_send()

            @pl.when(right_takes(c) & (origin <= w))
            def _():
                to_right(origin, c).wait_send()

        @pl.when(is_inner | (c < HOME))
        def _():
            out_copy(0, c).wait()

        @pl.when(is_inner & (c >= HOME))
        def _():
            back_copy(0, c).wait_send()

        @pl.when(is_end & (c >= HOME))
        def _():
            back_copy(0, c).wait_recv()

        return nothing

    lax.fori_loop(0, CHUNKS, finish, 0)

    @pl.when(is_end)
    def _():
        list_copy.wait_send()
        for p in range(TILE_PARTS):
            part_copy(p).wait_send()

    @pl.when(is_inner)
    def _():
        for p in range(TILE_PARTS):
            across_copy(p).wait_send()


def fused_shards(n_wide, amplitudes, integrals, tile_list, tile_counts):
    _, slab_rows, piece = amplitudes.shape
    slots, block = integrals.shape[2], integrals.shape[3]
    quarter_rows = slab_rows // 4
    step = quarter_rows // CHUNKS
    width = CB_DEV * block
    listed = tile_order(tile_list[0, 0], tile_counts[0, 0])
    anywhere = pl.BlockSpec(memory_space=pl.ANY)
    dma = pltpu.SemaphoreType.DMA
    result, _ = pl.pallas_call(
        functools.partial(ladder_kernel, n_wide),
        out_shape=(
            jax.ShapeDtypeStruct((quarter_rows, width), jnp.float32),
            jax.ShapeDtypeStruct(listed.shape, jnp.int32),
        ),
        in_specs=[pl.BlockSpec(memory_space=pltpu.SMEM)] + [anywhere] * 3,
        out_specs=(anywhere, anywhere),
        scratch_shapes=[
            pltpu.VMEM((4, quarter_rows, n_wide * piece), jnp.bfloat16),
            pltpu.VMEM((n_wide * piece // 128, 4, step, 128), jnp.bfloat16),
            pltpu.VMEM((slots, block, block), jnp.bfloat16),
            pltpu.VMEM((slots, block, block), jnp.bfloat16),
            pltpu.SMEM(listed.shape, jnp.int32),
            pltpu.VMEM((slots + 1, 4, step, block), jnp.float32),
            pltpu.VMEM((2, 2, step, width), jnp.float32),
            pltpu.VMEM((UNITS, 2, step, width), jnp.float32),
            pltpu.VMEM((3, 2, step, width), jnp.float32),
            pltpu.VMEM((2, step, width), jnp.float32),
            pltpu.VMEM((UNITS, step, width), jnp.float32),
            dma, dma, dma,
            dma((n_wide, CHUNKS)), dma((n_wide, CHUNKS)), dma((n_wide, CHUNKS)),
            dma((UNITS,)), dma((UNITS,)), dma((UNITS,)), dma((UNITS,)), dma((CHUNKS,)),
            dma((TILE_PARTS,)), dma((TILE_PARTS,)), dma((TILE_PARTS,)), dma((TILE_PARTS,)),
            dma, dma, dma((CHUNKS,)), dma((CHUNKS,)),
        ],
        compiler_params=pltpu.CompilerParams(
            collective_id=0, has_side_effects=True, vmem_limit_bytes=63 * 1024 * 1024
        ),
    )(listed, amplitudes.reshape(4, quarter_rows, piece), integrals[0, 0], listed)
    return result


def shards(sizes, amplitudes, integrals, tile_list, tile_counts):
    fits = (
        sizes["narrow"] == 2
        and sizes["sub"] == 2
        and sizes["wide"] == 4
        and sizes["groups"] == 2
        and amplitudes.shape[2] % 128 == 0
    )
    if fits:
        return fused_shards(sizes["wide"], amplitudes, integrals, tile_list, tile_counts)
    return gathered_shards(amplitudes, integrals, tile_list, tile_counts)


def solution(mesh):
    placed = (
        P(("narrow", "sub"), "groups", "wide"),
        P(("narrow", "sub"), "wide", None, None, None),
        P(("narrow", "sub"), "wide", None, None),
        P(("narrow", "sub"), "wide"),
    )
    return jax.shard_map(
        functools.partial(shards, dict(mesh.shape)),
        mesh=mesh,
        in_specs=placed,
        out_specs=P(("groups", "narrow", "sub"), "wide"),
        check_vma=False,
    )
```

time: 301 us -> 309 us (1.027)
  Pallas kernels: 293 us -> 301 us
    pallas_call x1, Pallas kernels: 293 us -> 301 us  [fused_shards(): pl.pallas_call(functools.partial(ladder_kernel, n_wide), out_shape=(jax.S...]
where the time goes in v2:
time: 309 us
  Pallas kernels  301 us (97%)
  local copies, waits for them, and re-layouts  4.9 us (2%)
    pallas_call x1, Pallas kernels, fused_shards(): pl.pallas_call(functools.partial(ladder_kernel, n_wide), out_shape=(jax.S...  301 us

profile of v2, /device:TPU:0, one launch (start us, length us, event | category | flops | bytes accessed | tf_op | source)
XLA Modules:
  0.0 308.6 jit_solution(17259132836170797934)
XLA Ops:
  0.7 0.7 iota_add_fusion
  1.3 0.8 slice_bitcast_fusion
  2.1 0.2 convert_reduce_fusion
  2.3 0.2 select_reduce_fusion.2
  2.5 0.1 convert_reduce_fusion.2
  2.6 0.6 pad.22.own_list.list_source
  3.2 301.1 %shard_map.46 = (f32[256,3840]{1,0:T(8,128)}, s32[8,128]{1,0:T(8,128)}) custom-call(s32[8,128]{1,0:T(8,128)} %pad.22.own_list.list_source, bf16[4,256,1920]{2,1,0:T(8,128)(2,1)} %bitcast.24, bf16[48,256,256]{2,1,0:T(8,128)(2,1)} %bitcast.23, s32[8,128]{1,0:T(8,128)} %pad.22.own_list.list_source), custom_call_target="tpu_custom_call" | custom-call | tf_op jit(solution)/shard_map/pallas_call | solution.py:383
  304.3 4.3 %copy.7 = f32[256,3840]{1,0:T(8,128)} copy(f32[256,3840]{1,0:T(8,128)} %get-tuple-element.6) | data formatting | bytes 7864320
  (7 shorter events, 0.0 us)

commit v3 on v2

--- a/solution.py
+++ b/solution.py
@@ -9,7 +9,8 @@
 
 CB_DEV = 15
 CHUNKS = 8
-HOME = 4
+HOME = 6
+LEAD = 4
 UNITS = HOME + 2 * (CHUNKS - HOME)
 TILE_PARTS = 4
 MESH = pl.DeviceIdType.MESH
@@ -166,6 +167,25 @@
         def _():
             to_right(w, c, amp.at[:, some(c), :]).start()
 
+    def pass_on(distance, c):
+        wanted = (c < HOME) | (is_inner & (c < CHUNKS))
+
+        @pl.when(wanted & (w + distance < n_wide))
+        def _():
+            to_left(w + distance, c).wait_recv()
+
+            @pl.when(left_takes(c))
+            def _():
+                to_left(w + distance, c).start()
+
+        @pl.when(wanted & (w - distance >= 0))
+        def _():
+            to_right(w - distance, c).wait_recv()
+
+            @pl.when(right_takes(c))
+            def _():
+                to_right(w - distance, c).start()
+
     def part_copy(p):
         here = pl.ds(g * (slots // 2) + p * part_slots, part_slots)
         return remote(
@@ -242,52 +262,42 @@
         list_copy.start()
         part_copy(0).start()
 
-    send_own(1)
+    for c in range(1, LEAD):
+        send_own(c)
     own_copy.wait()
     tile_copy.wait()
+    for c in range(n_wide - 2):
+        for distance in range(1, n_wide - 1 - c):
+            pass_on(distance, jnp.int32(c))
 
     def turn(u, nothing):
         c = chunk_of(u)
         opens = (u < HOME) | (lax.rem(u, 2) == 0)
 
-        @pl.when(opens & (c + 2 < CHUNKS))
-        def _():
-            send_own(c + 2)
+        @pl.when(opens & (c + LEAD < CHUNKS))
+        def _():
+            send_own(c + LEAD)
 
         @pl.when(is_end & (u + 1 < TILE_PARTS))
         def _():
             part_copy(u + 1).start()
 
-        @pl.when(is_inner & (u >= 1) & (u <= TILE_PARTS))
-        def _():
-            part_copy(u - 1).wait_recv()
-            across_copy(u - 1).start()
+        @pl.when(is_inner & (u >= HOME - TILE_PARTS) & (u < HOME))
+        def _():
+            part_copy(u - HOME + TILE_PARTS).wait_recv()
+            across_copy(u - HOME + TILE_PARTS).start()
 
         @pl.when(active(u) & opens)
         def _():
             for distance in range(1, n_wide):
-                @pl.when(w + distance < n_wide)
-                def _():
-                    to_left(w + distance, c).wait_recv()
-
-                    @pl.when(left_takes(c))
-                    def _():
-                        to_left(w + distance, c).start()
-
-                @pl.when(w - distance >= 0)
-                def _():
-                    to_right(w - distance, c).wait_recv()
-
-                    @pl.when(right_takes(c))
-                    def _():
-                        to_right(w - distance, c).start()
+                pass_on(distance, c + n_wide - 1 - distance)
 
             for half in range(2):
                 for place, quarter in ((half, 2 * half + 1 - s), (2 + half, 2 * half + s)):
                     for strip in range(strips):
                         mine[strip, place] = held[quarter, some(c), pl.ds(strip * 128, 128)]
 
-        @pl.when(is_inner & (u == TILE_PARTS))
+        @pl.when(is_inner & (u == HOME))
         def _():
             list_copy.wait_recv()
             to_list = pltpu.make_async_copy(list_landed, end_list, list_sem)

time: 309 us -> 249 us (0.81)
  Pallas kernels: 301 us -> 242 us
    pallas_call x1, Pallas kernels: 301 us -> 242 us  [fused_shards(): pl.pallas_call(functools.partial(ladder_kernel, n_wide), out_shape=(jax.S...]
where the time goes in v3:
time: 249 us
  Pallas kernels  242 us (97%)
  local copies, waits for them, and re-layouts  4.9 us (2%)
    pallas_call x1, Pallas kernels, fused_shards(): pl.pallas_call(functools.partial(ladder_kernel, n_wide), out_shape=(jax.S...  242 us

profile of v3, /device:TPU:0, one launch (start us, length us, event | category | flops | bytes accessed | tf_op | source)
XLA Modules:
  0.0 249.2 jit_solution(10815363941801490752)
XLA Ops:
  0.7 0.7 iota_add_fusion
  1.3 0.8 slice_bitcast_fusion
  2.1 0.2 convert_reduce_fusion
  2.3 0.2 select_reduce_fusion.2
  2.5 0.1 convert_reduce_fusion.2
  2.6 0.6 pad.22.own_list.list_source
  3.2 241.7 %shard_map.46 = (f32[256,3840]{1,0:T(8,128)}, s32[8,128]{1,0:T(8,128)}) custom-call(s32[8,128]{1,0:T(8,128)} %pad.22.own_list.list_source, bf16[4,256,1920]{2,1,0:T(8,128)(2,1)} %bitcast.24, bf16[48,256,256]{2,1,0:T(8,128)(2,1)} %bitcast.23, s32[8,128]{1,0:T(8,128)} %pad.22.own_list.list_source), custom_call_target="tpu_custom_call" | custom-call | tf_op jit(solution)/shard_map/pallas_call | solution.py:393
  244.9 4.3 %copy.7 = f32[256,3840]{1,0:T(8,128)} copy(f32[256,3840]{1,0:T(8,128)} %get-tuple-element.6) | data formatting | bytes 7864320
  (7 shorter events, 0.0 us)

commit v4 on v3

--- a/solution.py
+++ b/solution.py
@@ -10,7 +10,7 @@
 CB_DEV = 15
 CHUNKS = 8
 HOME = 6
-LEAD = 4
+LEAD = 5
 UNITS = HOME + 2 * (CHUNKS - HOME)
 TILE_PARTS = 4
 MESH = pl.DeviceIdType.MESH

time: 249 us -> 256 us (1.028)
  Pallas kernels: 242 us -> 248 us
    pallas_call x1, Pallas kernels: 242 us -> 248 us  [fused_shards(): pl.pallas_call(functools.partial(ladder_kernel, n_wide), out_shape=(jax.S...]
where the time goes in v4:
time: 256 us
  Pallas kernels  248 us (97%)
  local copies, waits for them, and re-layouts  4.9 us (2%)
    pallas_call x1, Pallas kernels, fused_shards(): pl.pallas_call(functools.partial(ladder_kernel, n_wide), out_shape=(jax.S...  248 us

profile of v4, /device:TPU:0, one launch (start us, length us, event | category | flops | bytes accessed | tf_op | source)
XLA Modules:
  0.0 255.5 jit_solution(12417831688667504750)
XLA Ops:
  0.7 0.7 iota_add_fusion
  1.3 0.8 slice_bitcast_fusion
  2.1 0.2 convert_reduce_fusion
  2.3 0.2 select_reduce_fusion.2
  2.5 0.1 convert_reduce_fusion.2
  2.6 0.6 pad.22.own_list.list_source
  3.2 248.0 %shard_map.46 = (f32[256,3840]{1,0:T(8,128)}, s32[8,128]{1,0:T(8,128)}) custom-call(s32[8,128]{1,0:T(8,128)} %pad.22.own_list.list_source, bf16[4,256,1920]{2,1,0:T(8,128)(2,1)} %bitcast.24, bf16[48,256,256]{2,1,0:T(8,128)(2,1)} %bitcast.23, s32[8,128]{1,0:T(8,128)} %pad.22.own_list.list_source), custom_call_target="tpu_custom_call" | custom-call | tf_op jit(solution)/shard_map/pallas_call | solution.py:393
  251.2 4.3 %copy.7 = f32[256,3840]{1,0:T(8,128)} copy(f32[256,3840]{1,0:T(8,128)} %get-tuple-element.6) | data formatting | bytes 7864320
  (7 shorter events, 0.0 us)
